TPU v7x, 512 devices: a whole 4x4x16 slice. The times are simulated.
512 devices in a mesh: row: 32 (over z_hi, y, core), col: 16 (over z_lo, x).
Axes of the slice: x: 4, y: 4, z: 16 (z_hi: 4, z_lo: 4; z = z_hi * 4 + z_lo), core: 2. Of those that a mesh axis runs over, the one named last changes fastest.
Arguments:
- objects: float32 [2, 2, 4096, 4096], P(None, None, 'row', 'col'), may hold values from -4 to 4
- illumination: float32 [2, 128, 128], replicated, may hold values from -4 to 4
- intensity: float32 [2048, 128, 128], P(('row', 'col')), may hold values from 0 to 2
- row_offset: int32 [2048], P(('row', 'col')), may hold values from 0 to 127
- col_offset: int32 [2048], P(('row', 'col')), may hold values from 0 to 255
Outputs:
- object_grad: float32 [2, 2, 4096, 4096], P(None, None, 'row', 'col')
- probe_grad: float32 [2, 128, 128], replicated
Inputs may be any that keep to these rules, and one draw needn't show every extreme that they name: `row_offset`: the row, within the tile of the device that holds position j, of the window's centre. `col_offset`: the column, within the tile of the device that holds position j, of the window's centre.
All inputs are finite; a program needn't handle non-finite values.
Results may differ from a plain program's by a relative error of at most 0.00013.
Values sent between devices are 32-bit elements; how exact they have to be, the bound alone decides.
A program may use at most 64 MiB of HBM per device.

v0:
```python
import math

import jax
import jax.numpy as jnp
from jax import lax
from jax.sharding import PartitionSpec as P

highest = lax.Precision.HIGHEST
depth = 0.5


def extended(block, sides, width):
    for axis, dim in sides:
        count = lax.axis_size(axis)
        forward = [(i, i + 1) for i in range(count - 1)]
        backward = [(target, source) for source, target in forward]
        low = lax.ppermute(
            lax.slice_in_dim(block, block.shape[dim] - width, None, axis=dim), axis, forward
        )
        high = lax.ppermute(lax.slice_in_dim(block, 0, width, axis=dim), axis, backward)
        block = jnp.concatenate([low, block, high], axis=dim)
    return block


def fourier_tables(length):
    index = jnp.arange(length, dtype=jnp.int32)
    product_index = index[:, None] * index[None, :] % length
    angle = -2.0 * math.pi / length * product_index.astype(jnp.float32)
    factor = 1.0 / math.sqrt(length)
    return (jnp.cos(angle) * factor, jnp.sin(angle) * factor)


def fresnel_pair(length):
    index = jnp.arange(length, dtype=jnp.int32)
    signed = jnp.where(index < length // 2, index, index - length)
    square = signed[:, None] ** 2 + signed[None, :] ** 2
    angle = -math.pi * depth / length * square.astype(jnp.float32)
    return jnp.stack([jnp.cos(angle), jnp.sin(angle)])


def real_part(values):
    return values[..., 0, :, :]


def imag_part(values):
    return values[..., 1, :, :]


def paired(real_value, imag_value):
    return jnp.stack([real_value, imag_value], axis=-3)


def product(left_field, right_field):
    real_value = real_part(left_field) * real_part(right_field) - imag_part(left_field) * imag_part(
        right_field
    )
    imag_value = real_part(left_field) * imag_part(right_field) + imag_part(left_field) * real_part(
        right_field
    )
    return paired(real_value, imag_value)


def conjugate(values):
    return paired(real_part(values), -imag_part(values))


def spectrum(values, cosine, sine):
    with_cos = jnp.einsum("...jk,kl->...jl", values, cosine, precision=highest)
    with_sin = jnp.einsum("...jk,kl->...jl", values, sine, precision=highest)
    middle = paired(
        real_part(with_cos) - imag_part(with_sin), real_part(with_sin) + imag_part(with_cos)
    )
    with_cos = jnp.einsum("ij,...jk->...ik", cosine, middle, precision=highest)
    with_sin = jnp.einsum("ij,...jk->...ik", sine, middle, precision=highest)
    return paired(
        real_part(with_cos) - imag_part(with_sin), real_part(with_sin) + imag_part(with_cos)
    )


def fold_rows(values, half_size):
    height = values.shape[2]
    edges = jnp.concatenate([values[:, :, :half_size], values[:, :, height - half_size :]], axis=2)
    arrived = extended(edges, (("row", 2),), half_size)
    inside = values[:, :, half_size : height - half_size]
    inside = inside.at[:, :, :half_size].add(arrived[:, :, :half_size])
    return inside.at[:, :, inside.shape[2] - half_size :].add(arrived[:, :, 3 * half_size :])


def fold_cols(values, half_size):
    width = values.shape[3]
    edges = jnp.concatenate(
        [values[:, :, :, :half_size], values[:, :, :, width - half_size :]], axis=3
    )
    arrived = extended(edges, (("col", 3),), half_size)
    inside = values[:, :, :, half_size : width - half_size]
    inside = inside.at[:, :, :, :half_size].add(arrived[:, :, :, :half_size])
    return inside.at[:, :, :, inside.shape[3] - half_size :].add(arrived[:, :, :, 3 * half_size :])


def on_device(objects, illumination, intensity, row_offset, col_offset):
    length = illumination.shape[-1]
    half_size = length // 2
    count = row_offset.shape[0]
    cosine, sine = fourier_tables(length)
    fresnel = fresnel_pair(length)
    anchor = jnp.zeros((), jnp.int32)

    def windows_of(padded):

        def one_window(start_row, start_col):
            return lax.dynamic_slice(padded, (anchor, start_row, start_col), (2, length, length))

        return jax.vmap(one_window)(row_offset, col_offset)

    padded_both = extended(objects, (("row", 2), ("col", 3)), half_size)
    first_window = windows_of(padded_both[0])
    second_window = windows_of(padded_both[1])
    entry = product(illumination, first_window)
    moved = spectrum(product(spectrum(entry, cosine, sine), fresnel), cosine, -sine)
    exit_wave = product(moved, second_window)
    far_field = spectrum(exit_wave, cosine, sine)
    residual = real_part(far_field) ** 2 + imag_part(far_field) ** 2 - intensity
    far_grad = far_field * residual[:, None]
    exit_grad = spectrum(far_grad, cosine, -sine)
    moved_grad = product(conjugate(second_window), exit_grad)
    second_grad = product(conjugate(moved), exit_grad)
    entry_grad = spectrum(
        product(spectrum(moved_grad, cosine, sine), conjugate(fresnel)), cosine, -sine
    )
    first_grad = product(conjugate(illumination), entry_grad)
    probe_local = jnp.sum(product(conjugate(first_window), entry_grad), axis=0)
    stacked = jnp.stack([first_grad, second_grad], axis=1)
    padded_height = objects.shape[2] + 2 * half_size
    padded_width = objects.shape[3] + 2 * half_size

    def place(number, running):
        corner = (anchor, anchor, row_offset[number], col_offset[number])
        previous = lax.dynamic_slice(running, corner, (2, 2, length, length))
        return lax.dynamic_update_slice(running, previous + stacked[number], corner)

    total = lax.fori_loop(
        0, count, place, jnp.zeros((2, 2, padded_height, padded_width), jnp.float32)
    )
    object_grad = fold_cols(fold_rows(total, half_size), half_size)
    probe_total = lax.psum(probe_local, ("row", "col"))
    positions = count * lax.axis_size("row") * lax.axis_size("col")
    return (object_grad, probe_total / math.sqrt(positions))


def solution(mesh):
    return jax.shard_map(
        on_device,
        mesh=mesh,
        in_specs=(
            P(None, None, "row", "col"),
            P(),
            P(("row", "col"), None, None),
            P(("row", "col")),
            P(("row", "col")),
        ),
        out_specs=(P(None, None, "row", "col"), P()),
        check_vma=False,
    )
```

profile of v0, /device:TPU:1, one launch (start us, length us, event | category | flops | bytes accessed | tf_op | source)
XLA Modules:
  0.0 610.8 jit_solution(8579191948747801594)
XLA Ops:
  7.2 1.1 fusion.206
  8.4 4.6 collective-permute-start
  13.0 5.5 collective-permute-start.1
  19.6 1.1 collective-permute-done.1
  20.7 1.0 fusion.204
  21.7 3.1 collective-permute-start.2
  24.8 1.3 collective-permute-start.3
  27.3 7.2 %collective-permute-done.2 = f32[2,2,256,64]{3,2,1,0:T(8,128)S(1)} collective-permute-done((f32[2,2,256,64]{3,2,1,0:T(8,128)}, f32[2,2,256,64]{3,2,1,0:T(8,128)S(1)}, u32[]{:S(2)}, u32[]{:S(2)}) %collective-permute-start.2) | collective-permute-done | bytes 262176 | tf_op jit(solution)/shard_map/ppermute | solution.py:17
  34.5 3.8 collective-permute-done.3
  39.1 8.2 %while.21 = (s32[]{:T(128)}, f32[2,256,384]{2,1,0:T(8,128)S(1)}, s32[4,3]{1,0:T(4,128)S(1)}, f32[4,2,128,128]{3,2,1,0:T(8,128)S(1)}, s32[]{:T(128)}) while((s32[]{:T(128)}, f32[2,256,384]{2,1,0:T(8,128)S(1)}, s32[4,3]{1,0:T(4,128)S(1)}, f32[4,2,128,128]{3,2,1,0:T(8,128)S(1)}, s32[]{:T(128)}) %tuple.113), condition=%wide.while_cond.5, body=%wide.while_body.5.sunk | while | flops 2 | bytes 262261 | solution.py:111
  39.8 1.4 bitcast_dynamic-update-slice_fusion.5
  41.8 1.4 bitcast_dynamic-update-slice_fusion.5
  43.9 1.4 bitcast_dynamic-update-slice_fusion.5
  45.9 1.4 bitcast_dynamic-update-slice_fusion.5
  49.1 1.1 convolution_bitcast_fusion.11
  50.2 1.1 convolution_bitcast_fusion.10
  51.4 1.1 fusion.7
  52.6 1.1 fusion.6
  55.6 8.2 %while.20 = (s32[]{:T(128)}, f32[2,256,384]{2,1,0:T(8,128)S(1)}, s32[4,3]{1,0:T(4,128)S(1)}, f32[4,2,128,128]{3,2,1,0:T(8,128)S(1)}, s32[]{:T(128)}) while((s32[]{:T(128)}, f32[2,256,384]{2,1,0:T(8,128)S(1)}, s32[4,3]{1,0:T(4,128)S(1)}, f32[4,2,128,128]{3,2,1,0:T(8,128)S(1)}, s32[]{:T(128)}) %tuple.121), condition=%wide.while_cond.4, body=%wide.while_body.4.sunk | while | flops 2 | bytes 262261 | solution.py:111
  56.2 1.4 bitcast_dynamic-update-slice_fusion.4
  58.2 1.4 bitcast_dynamic-update-slice_fusion.4
  60.2 1.4 bitcast_dynamic-update-slice_fusion.4
  62.2 1.4 bitcast_dynamic-update-slice_fusion.4
  65.7 1.1 convolution_bitcast_fusion.7
  66.8 1.1 convolution_bitcast_fusion.6
  68.0 1.2 fusion.11
  69.2 1.2 fusion.10
  74.1 1.1 convolution_bitcast_fusion.3
  75.3 1.3 convolution_bitcast_fusion.2
  76.7 1.1 fusion.1
  77.8 1.1 fusion
  81.8 33.4 %while.19 = (s32[]{:T(128)}, f32[2,2,256,384]{3,2,1,0:T(8,128)S(1)}, s32[4]{0:T(128)S(1)}, s32[4]{0:T(128)S(1)}, f32[4,2,2,128,128]{4,3,2,0,1:T(8,128)S(1)}, /*index=5*/s32[]{:T(128)}, s32[]{:T(128)}, s32[]{:T(128)}, s32[]{:T(128)}) while((s32[]{:T(128)}, f32[2,2,256,384]{3,2,1,0:T(8,128)S(1)}, s32[4]{0:T(128)S(1)}, s32[4]{0:T(128)S(1)}, ...), condition=%wide.region_1.2_spmd, body=%wide.region_0.1_spmd.sunk | while | flops 65544 | bytes 1310921 | solution.py:141
  87.0 3.2 dynamic_update_slice.8
  95.4 3.1 dynamic_update_slice.8
  103.8 3.1 dynamic_update_slice.8
  112.1 3.0 dynamic_update_slice.8
  116.1 5.2 collective-permute-start.4
  121.3 1.9 collective-permute-start.5
  124.0 2.3 collective-permute-done.4
  126.3 1.0 add_dynamic-update-slice_fusion
  127.4 3.4 collective-permute-done.5
  130.7 1.1 fusion.12
  131.9 2.9 collective-permute-start.6
  134.8 455.2 %all-reduce.2.cloned.1.call-done = f32[2,128,128]{2,1,0:T(8,128)} async-done(((f32[2,128,128]{2,1,0:T(8,128)}), f32[2,128,128]{2,1,0:T(8,128)}) %all-reduce.2.cloned.1.call-update) | async-done | bytes 131088 | tf_op jit(solution)/shard_map/psum | solution.py:145
  590.0 1.6 broadcast_multiply_fusion
  591.8 1.3 collective-permute-start.7
  593.9 7.9 %collective-permute-done.7 = f32[2,2,128,64]{3,2,1,0:T(8,128)S(1)} collective-permute-done((f32[2,2,128,64]{3,2,1,0:T(8,128)S(1)}, f32[2,2,128,64]{3,2,1,0:T(8,128)S(1)}, u32[]{:S(2)}, u32[]{:S(2)}) %collective-permute-start.7) | collective-permute-done | bytes 131104 | tf_op jit(solution)/shard_map/ppermute | solution.py:20
  601.9 1.3 scatter-add.19
  (97 shorter events, 29.3 us)
Async XLA Ops:
  7.2 12.3 %copy-start = (f32[2,2,128,256]{3,2,1,0:T(8,128)S(1)}, f32[2,2,128,256]{3,2,1,0:T(8,128)}, u32[]{:S(2)}) copy-start(f32[2,2,128,256]{3,2,1,0:T(8,128)} %param.15) | copy-start | bytes 1572868
  7.2 582.8 %all-reduce.2.cloned.1.call-start = ((), (), s32[]{:S(2)}) async-start(), calls=%async_computation | async-start | bytes 262144 | tf_op jit(solution)/shard_map/psum | solution.py:145
  8.4 11.1 %collective-permute-start = (f32[2,2,64,256]{3,2,1,0:T(8,128)S(1)}, f32[2,2,64,256]{3,2,1,0:T(8,128)S(1)}, u32[]{:S(2)}, u32[]{:S(2)}) collective-permute-start(f32[2,2,64,256]{3,2,1,0:T(8,128)S(1)} %get-tuple-element.249), channel_id=1, source_target_pairs={{0,16},{16,32},{32,48},{48,64},{64,80},{80,96},{96,112},{112,128},... | collective-permute-start | bytes 786440 | tf_op jit(solution)/shard_map/ppermute | solution.py:17
  13.0 7.7 %collective-permute-start.1 = (f32[2,2,64,256]{3,2,1,0:T(8,128)S(1)}, f32[2,2,64,256]{3,2,1,0:T(8,128)S(1)}, u32[]{:S(2)}, u32[]{:S(2)}) collective-permute-start(f32[2,2,64,256]{3,2,1,0:T(8,128)S(1)} %get-tuple-element.248), channel_id=1, source_target_pairs={{16,0},{32,16},{48,32},{64,48},{80,64},{96,80},{112,96},{128,112},... | collective-permute-start | bytes 786440 | tf_op jit(solution)/shard_map/ppermute | solution.py:20
  19.6 6.7 %copy-start.2 = (f32[4,128,128]{2,1,0:T(8,128)S(1)}, f32[4,128,128]{2,1,0:T(8,128)}, u32[]{:S(2)}) copy-start(f32[4,128,128]{2,1,0:T(8,128)} %param.17) | copy-start | bytes 786436
  21.7 12.8 %collective-permute-start.2 = (f32[2,2,256,64]{3,2,1,0:T(8,128)}, f32[2,2,256,64]{3,2,1,0:T(8,128)S(1)}, u32[]{:S(2)}, u32[]{:S(2)}) collective-permute-start(f32[2,2,256,64]{3,2,1,0:T(8,128)} %get-tuple-element.238), channel_id=1, source_target_pairs={{0,1},{1,2},{2,3},{3,4},{4,5},{5,6},{6,7},{7,8},{8,9},{9,10},{10,1... | collective-permute-start | bytes 786440 | tf_op jit(solution)/shard_map/ppermute | solution.py:17
  24.8 13.5 %collective-permute-start.3 = (f32[2,2,256,64]{3,2,1,0:T(8,128)S(1)}, f32[2,2,256,64]{3,2,1,0:T(8,128)S(1)}, u32[]{:S(2)}, u32[]{:S(2)}) collective-permute-start(f32[2,2,256,64]{3,2,1,0:T(8,128)S(1)} %get-tuple-element.239), channel_id=1, source_target_pairs={{1,0},{2,1},{3,2},{4,3},{5,4},{6,5},{7,6},{8,7},{9,8},{10,9},{11,1... | collective-permute-start | bytes 786440 | tf_op jit(solution)/shard_map/ppermute | solution.py:20
  81.1 0.7 copy-start.3
  81.1 0.7 copy-start.4
  116.1 10.2 %collective-permute-start.4 = (f32[2,2,64,384]{3,2,1,0:T(8,128)}, f32[2,2,64,384]{3,2,1,0:T(8,128)}, u32[]{:S(2)}, u32[]{:S(2)}) collective-permute-start(f32[2,2,64,384]{3,2,1,0:T(8,128)} %get-tuple-element.217), channel_id=1, source_target_pairs={{0,16},{16,32},{32,48},{48,64},{64,80},{80,96},{96,112},{112,128},... | collective-permute-start | bytes 1179656 | tf_op jit(solution)/shard_map/ppermute | solution.py:17
  121.3 9.4 %collective-permute-start.5 = (f32[2,2,64,384]{3,2,1,0:T(8,128)}, f32[2,2,64,384]{3,2,1,0:T(8,128)}, u32[]{:S(2)}, u32[]{:S(2)}) collective-permute-start(f32[2,2,64,384]{3,2,1,0:T(8,128)} %get-tuple-element.216), channel_id=1, source_target_pairs={{16,0},{32,16},{48,32},{64,48},{80,64},{96,80},{112,96},{128,112},... | collective-permute-start | bytes 1179656 | tf_op jit(solution)/shard_map/ppermute | solution.py:20
  131.9 461.1 %collective-permute-start.6 = (f32[2,2,128,64]{3,2,1,0:T(8,128)S(1)}, f32[2,2,128,64]{3,2,1,0:T(8,128)S(1)}, u32[]{:S(2)}, u32[]{:S(2)}) collective-permute-start(f32[2,2,128,64]{3,2,1,0:T(8,128)S(1)} %get-tuple-element.241), channel_id=1, source_target_pairs={{0,1},{1,2},{2,3},{3,4},{4,5},{5,6},{6,7},{7,8},{8,9},{9,10},{10,1... | collective-permute-start | bytes 393224 | tf_op jit(solution)/shard_map/ppermute | solution.py:17
  591.8 10.0 %collective-permute-start.7 = (f32[2,2,128,64]{3,2,1,0:T(8,128)S(1)}, f32[2,2,128,64]{3,2,1,0:T(8,128)S(1)}, u32[]{:S(2)}, u32[]{:S(2)}) collective-permute-start(f32[2,2,128,64]{3,2,1,0:T(8,128)S(1)} %get-tuple-element.240), channel_id=1, source_target_pairs={{1,0},{2,1},{3,2},{4,3},{5,4},{6,5},{7,6},{8,7},{9,8},{10,9},{11,1... | collective-permute-start | bytes 393224 | tf_op jit(solution)/shard_map/ppermute | solution.py:20
  603.2 0.8 copy-start.1
Sparse Core Ops, SparseCore 0:
  124.1 465.8 all-reduce.1
where the time goes:
time: 612 us; the launch traced here: 611 us
  waiting for transfers between devices  481 us (79%)
  local copies, waits for them, and re-layouts  40.4 us (7%)
  starting transfers between devices  25.8 us (4%)
  matrix products  24 us (4%)
  loops' own time  16.1 us (3%)
  between operations  14.6 us (2%)
  other arithmetic  9.12 us (1%)
    psum x1, waiting for transfers between devices, on_device(): probe_total = lax.psum(probe_local, ('row', 'col'))  455 us
    ppermute x4, waiting for transfers between devices, extended(): lax.ppermute(lax.slice_in_dim(block, 0, width, axis=dim), axis, backward)  16.1 us
    gather x24, local copies, waits for them, and re-layouts  16 us
    ppermute x4, starting transfers between devices, extended(): lax.ppermute(lax.slice_in_dim(block, block.shape[dim] - width, None, axis...  15.8 us
    another operation x1, loops' own time, on_device(): lax.fori_loop(0, count, place, jnp.zeros((2, 2, padded_height, padded_wid...  15.7 us
    dynamic_update_slice x4, local copies, waits for them, and re-layouts, place(): return lax.dynamic_update_slice(running, previous + stacked[number], corner)  12.4 us
  transfers between devices with their start and end apart: 9, of which 7 were waited for; matrix products, arithmetic and copies ran while one was open for 1% of the time, Pallas kernels for 0%

commit v1 on v0

v1 whole, which is shorter than its diff:
```python
import functools
import math

import jax
import jax.numpy as jnp
import ml_dtypes
import numpy as np
from jax import lax
from jax.experimental import pallas as pl
from jax.experimental.pallas import tpu as pltpu
from jax.sharding import PartitionSpec as P

depth = 0.5
side = 128
half = 64
tile_w = 256
count = 4
plane_rows = 8
plane_cols = 4
directions = ((-1, 0), (1, 0), (0, -1), (0, 1), (-1, -1), (-1, 1), (1, -1), (1, 1))
MESH = pl.DeviceIdType.MESH
f32 = jnp.float32
bf16 = jnp.bfloat16


def in_two(values):
    high = values.astype(ml_dtypes.bfloat16)
    low = (values - high.astype(np.float64)).astype(ml_dtypes.bfloat16)
    return high, low


def tables():
    index = np.arange(side)
    angle = -2.0 * math.pi / side * (index[:, None] * index[None, :] % side)
    real, imag = np.cos(angle) / math.sqrt(side), np.sin(angle) / math.sqrt(side)
    rows = np.block([[real, imag], [-imag, real]])
    cols = np.block([[real, -imag], [imag, real]])
    signed = np.where(index < side // 2, index, index - side)
    square = signed[:, None] ** 2 + signed[None, :] ** 2
    phase = -math.pi * depth / side * square
    fresnel = np.stack([np.cos(phase), np.sin(phase)]).astype(np.float32)
    return np.stack(in_two(rows) + in_two(cols)), fresnel


def split(values):
    high = values.astype(bf16)
    return high, (values - high.astype(f32)).astype(bf16)


def dot(left, right):
    return lax.dot_general(left, right, (((1,), (0,)), ((), ())), preferred_element_type=f32)


def kernel(
    mesh_shape,
    row_ref,
    col_ref,
    obj_ref,
    ill_ref,
    int_ref,
    tab_ref,
    fres_ref,
    og_ref,
    pg_ref,
    pad0,
    pad1,
    east_src,
    west_src,
    east_in,
    west_in,
    ill,
    inten,
    tab,
    fres,
    first_w,
    second_w,
    moved_s,
    acc0,
    acc1,
    fe_src,
    fw_src,
    ns_in,
    fe_in,
    fw_in,
    og,
    ar_src,
    ar_in,
    z_in,
    ar_out,
    local_sem,
    halo_send,
    halo_recv,
    fold_send,
    fold_recv,
    ar_send,
    ar_recv,
):
    n_row, n_col = mesh_shape
    row, col = lax.axis_index("row"), lax.axis_index("col")
    pads, accs = (pad0, pad1), (acc0, acc1)

    own = [
        [
            pltpu.make_async_copy(
                obj_ref.at[s, :, :, t * side : (t + 1) * side],
                pads[s].at[t + 1, :, half : half + side],
                local_sem.at[2 * s + t],
            )
            for t in range(2)
        ]
        for s in range(2)
    ]
    loads = [
        pltpu.make_async_copy(ill_ref, ill, local_sem.at[4]),
        pltpu.make_async_copy(tab_ref, tab, local_sem.at[5]),
        pltpu.make_async_copy(fres_ref, fres, local_sem.at[6]),
        pltpu.make_async_copy(int_ref, inten, local_sem.at[7]),
    ]
    for copy in own[0] + own[1] + loads:
        copy.start()

    def has(dr, dc):
        found = None
        if dr:
            found = (row > 0) if dr < 0 else (row < n_row - 1)
        if dc:
            col_found = (col > 0) if dc < 0 else (col < n_col - 1)
            found = col_found if found is None else jnp.logical_and(found, col_found)
        return found

    def halo_dst(s, dr, dc):
        if dc == 0:
            start = 3 * half if dr < 0 else 0
            return pads[s].at[1:3, :, start : start + half]
        into = west_in if dc > 0 else east_in
        start, size = ((half, side) if dr == 0 else (3 * half, half) if dr < 0 else (0, half))
        return into.at[s, start : start + size]

    def halo_copy(s, d):
        dr, dc = directions[d]
        if dc == 0:
            start = half if dr < 0 else side
            src = pads[s].at[1:3, :, start : start + half]
        else:
            start, size = ((0, side) if dr == 0 else (0, half) if dr < 0 else (half, half))
            src = (east_src if dc > 0 else west_src).at[s, start : start + size]
        return pltpu.make_async_remote_copy(
            src_ref=src,
            dst_ref=halo_dst(s, dr, dc),
            send_sem=halo_send.at[s, d],
            recv_sem=halo_recv.at[s, d],
            device_id=(row + dr, col + dc),
            device_id_type=MESH,
        )

    def fold_dst(s, dr, dc):
        if dc == 0:
            return ns_in.at[s, 1 if dr < 0 else 0]
        into = fw_in if dc > 0 else fe_in
        start, size = ((0, side) if dr == 0 else (3 * half, half) if dr < 0 else (side, half))
        return into.at[s, start : start + size]

    def fold_copy(s, d):
        dr, dc = directions[d]
        start, size = ((half, side) if dr == 0 else (0, half) if dr < 0 else (3 * half, half))
        if dc == 0:
            src = accs[s].at[:, start : start + size, 0:tile_w]
        else:
            src = (fe_src if dc > 0 else fw_src).at[s, start : start + size]
        return pltpu.make_async_remote_copy(
            src_ref=src,
            dst_ref=fold_dst(s, dr, dc),
            send_sem=fold_send.at[s, d],
            recv_sem=fold_recv.at[s, d],
            device_id=(row + dr, col + dc),
            device_id_type=MESH,
        )

    for dr, dc in directions:

        @pl.when(jnp.logical_not(has(-dr, -dc)))
        def _(dr=dr, dc=dc):
            for s in range(2):
                for dst in (halo_dst(s, dr, dc), fold_dst(s, dr, dc)):
                    dst[...] = jnp.zeros(dst.shape, f32)

    inner, outer = plane_rows * plane_cols, (n_row // plane_rows) * (n_col // plane_cols)
    outer_cols = n_col // plane_cols
    row_in, row_out = lax.rem(row, plane_rows), lax.div(row, plane_rows)
    col_in, col_out = lax.rem(col, plane_cols), lax.div(col, plane_cols)
    my_inner = row_in * plane_cols + col_in
    my_outer = row_out * outer_cols + col_out

    def inner_device(k):
        number = lax.rem(my_inner + k, inner)
        return number, (
            row_out * plane_rows + lax.div(number, plane_cols),
            col_out * plane_cols + lax.rem(number, plane_cols),
        )

    def outer_device(k):
        number = lax.rem(my_outer + k, outer)
        return number, (
            lax.div(number, outer_cols) * plane_rows + row_in,
            lax.rem(number, outer_cols) * plane_cols + col_in,
        )

    barrier = pltpu.get_barrier_semaphore()
    expected = jnp.int32(inner + outer - 2)
    for dr, dc in directions:
        found = has(dr, dc)
        expected = expected + found.astype(jnp.int32)

        @pl.when(found)
        def _(dr=dr, dc=dc):
            pl.semaphore_signal(
                barrier, inc=1, device_id=(row + dr, col + dc), device_id_type=MESH
            )

    def greet(device_of):
        def step(k, carry):
            pl.semaphore_signal(barrier, inc=1, device_id=device_of(k)[1], device_id_type=MESH)
            return carry

        return step

    lax.fori_loop(1, inner, greet(inner_device), 0)
    lax.fori_loop(1, outer, greet(outer_device), 0)

    def send_all(copy_of):
        for d in range(8):

            @pl.when(has(*directions[d]))
            def _(d=d):
                copy_of(d).start()

    def receive_all(copy_of):
        for d in range(8):
            dr, dc = directions[d]

            @pl.when(has(-dr, -dc))
            def _(d=d):
                copy_of(d).wait_recv()

    def sent_all(copy_of):
        for d in range(8):

            @pl.when(has(*directions[d]))
            def _(d=d):
                copy_of(d).wait_send()

    lane = lax.broadcasted_iota(jnp.int32, (1, side), 1)
    lower = lane < half

    def pack_edges(s):
        for copy in own[s]:
            copy.wait()
        rows = slice(half, half + side)
        west_src[s] = jnp.where(
            lower, pads[s][1, 0, rows], pltpu.roll(pads[s][1, 1, rows], half, 1)
        )
        east_src[s] = jnp.where(
            lower, pltpu.roll(pads[s][2, 1, rows], half, 1), pads[s][2, 0, rows]
        )

    pack_edges(0)
    pl.semaphore_wait(barrier, expected)
    send_all(lambda d: halo_copy(0, d))
    pack_edges(1)
    send_all(lambda d: halo_copy(1, d))

    row_at = [row_ref[j] for j in range(count)]
    col_at = [col_ref[j] for j in range(count)]
    row_grid = lax.broadcasted_iota(jnp.int32, (2 * side, side), 0)
    col_grid = lax.broadcasted_iota(jnp.int32, (2 * side, side), 1)
    place_rows = jnp.concatenate(
        [
            jnp.where(row_grid - col_grid == row_at[j], 1.0, 0.0).astype(bf16)
            for j in range(count)
        ],
        axis=1,
    )

    def lane_mask(j, k):
        offset = lane + (side * k + half) - col_at[j]
        offset = jnp.where(offset < 0, offset + 3 * side, offset)
        offset = jnp.where(offset >= 3 * side, offset - 3 * side, offset)
        return jnp.where(offset < side, 1.0, 0.0).astype(bf16)

    def join_halo(s):
        east, west = east_in[s], west_in[s]
        halo = (
            jnp.where(lower, east, west),
            pltpu.roll(jnp.where(lower, west, east), half, 1),
        )
        for part in range(2):
            pads[s][0, part] = halo[part]
            pads[s][3, part] = halo[part]

    def gather(s, out):
        for j in range(count):
            start = col_at[j] + half
            tile = lax.div(start, side)
            shift = lax.rem(start, side)
            back = lax.rem(side - shift, side)
            for part in range(2):
                near = pads[s][tile, part, pl.ds(row_at[j], side)]
                far = pads[s][tile + 1, part, pl.ds(row_at[j], side)]
                out[j * side : (j + 1) * side, part * side : (part + 1) * side] = pltpu.roll(
                    jnp.where(lane >= shift, near, far), back, 1
                )

    def by_rows(values, inverse=False):
        k = 2 if inverse else 0
        high, low = split(values)
        return dot(high, tab[k]) + dot(low, tab[k]) + dot(high, tab[k + 1])

    def by_cols(values, inverse=False):
        k = 0 if inverse else 2
        high, low = split(values)
        return dot(tab[k], high) + dot(tab[k], low) + dot(tab[k + 1], high)

    def stand(values):
        return jnp.concatenate(
            [
                jnp.concatenate(
                    [
                        values[j * side : (j + 1) * side, part * side : (part + 1) * side]
                        for j in range(count)
                    ],
                    axis=1,
                )
                for part in range(2)
            ],
            axis=0,
        )

    def lie(values):
        return jnp.concatenate(
            [
                jnp.concatenate(
                    [
                        values[part * side : (part + 1) * side, j * side : (j + 1) * side]
                        for part in range(2)
                    ],
                    axis=1,
                )
                for j in range(count)
            ],
            axis=0,
        )

    def real(values):
        return values[:, :side]

    def imag(values):
        return values[:, side:]

    def times(left, right):
        return jnp.concatenate(
            [
                real(left) * real(right) - imag(left) * imag(right),
                real(left) * imag(right) + imag(left) * real(right),
            ],
            axis=1,
        )

    def conj_times(left, right):
        return jnp.concatenate(
            [
                real(left) * real(right) + imag(left) * imag(right),
                real(left) * imag(right) - imag(left) * real(right),
            ],
            axis=1,
        )

    def propagate(values, sign):
        spectrum = by_cols(stand(by_rows(values)))
        h_real = jnp.concatenate([fres[0]] * count, axis=1)
        h_imag = jnp.concatenate([fres[1]] * count, axis=1) * sign
        s_real, s_imag = spectrum[:side], spectrum[side:]
        spectrum = jnp.concatenate(
            [s_real * h_real - s_imag * h_imag, s_real * h_imag + s_imag * h_real], axis=0
        )
        return by_rows(lie(by_cols(spectrum, True)), True)

    def place(s, values):
        pieces = ([], [])
        for j in range(count):
            start = lax.rem(col_at[j] + half, side)
            masks = [lane_mask(j, k) for k in range(3)]
            for part in range(2):
                window = values[j * side : (j + 1) * side, part * side : (part + 1) * side]
                for piece, block in zip(pieces, split(pltpu.roll(window, start, 1))):
                    piece.append(jnp.concatenate([block * m for m in masks], axis=1))
        total = None
        for piece in pieces:
            both = jnp.concatenate(
                [
                    jnp.concatenate([piece[2 * j], piece[2 * j + 1]], axis=1)
                    for j in range(count)
                ],
                axis=0,
            )
            part_sum = dot(place_rows, both)
            total = part_sum if total is None else total + part_sum
        accs[s][0] = total[:, : 3 * side]
        accs[s][1] = total[:, 3 * side :]
        halo_real, halo_imag = total[:, 2 * side : 3 * side], total[:, 5 * side :]
        turned = pltpu.roll(halo_imag, half, 1)
        fe_src[s] = jnp.where(lower, halo_real, turned)
        fw_src[s] = jnp.where(lower, turned, halo_real)

    def finish(s):
        from_west = fw_in[s, 0:side] + fw_in[s, side : 2 * side]
        from_east = fe_in[s, 0:side] + fe_in[s, side : 2 * side]
        for part in range(2):
            if part:
                from_west = pltpu.roll(from_west, half, 1)
                from_east = pltpu.roll(from_east, half, 1)
            rows = slice(half, half + side)
            above_below = jnp.concatenate([ns_in[s, 0, part], ns_in[s, 1, part]], axis=0)
            og[s, part, :, 0:side] = (
                accs[s][part, rows, 0:side]
                + above_below[:, 0:side]
                + jnp.where(lower, from_west, 0.0)
            )
            og[s, part, :, side:tile_w] = (
                accs[s][part, rows, side:tile_w]
                + above_below[:, side:tile_w]
                + jnp.where(lower, 0.0, from_east)
            )
        out_copy(s).start()

    def out_copy(s):
        return pltpu.make_async_copy(og.at[s], og_ref.at[s], local_sem.at[s])

    for copy in loads[:3]:
        copy.wait()
    illumination = jnp.concatenate([ill[0], ill[1]], axis=1)
    probe = jnp.concatenate([illumination] * count, axis=0)

    receive_all(lambda d: halo_copy(0, d))
    join_halo(0)
    gather(0, first_w)
    moved_s[...] = propagate(times(probe, first_w[...]), 1.0)

    receive_all(lambda d: halo_copy(1, d))
    join_halo(1)
    gather(1, second_w)
    far = by_cols(stand(by_rows(times(moved_s[...], second_w[...]))))
    loads[3].wait()
    measured = jnp.concatenate([inten[j] for j in range(count)], axis=1)
    far_real, far_imag = far[:side], far[side:]
    residual = far_real * far_real + far_imag * far_imag - measured
    far_grad = jnp.concatenate([far_real * residual, far_imag * residual], axis=0)
    exit_grad = by_rows(lie(by_cols(far_grad, True)), True)

    place(1, conj_times(moved_s[...], exit_grad))
    send_all(lambda d: fold_copy(1, d))

    entry_grad = propagate(conj_times(second_w[...], exit_grad), -1.0)
    probe_local = conj_times(first_w[...], entry_grad)
    probe_local = sum(probe_local[j * side : (j + 1) * side] for j in range(count))
    ar_src[0:side] = real(probe_local)
    ar_src[side : 2 * side] = imag(probe_local)

    chunk = 2 * side // inner

    def rows_of(number):
        return pl.ds(pl.multiple_of(number * chunk, chunk), chunk)

    def scatter_copy(k):
        number, device = inner_device(k)
        return pltpu.make_async_remote_copy(
            src_ref=ar_src.at[rows_of(number)],
            dst_ref=ar_in.at[rows_of(my_inner)],
            send_sem=ar_send.at[0],
            recv_sem=ar_recv.at[0],
            device_id=device,
            device_id_type=MESH,
        )

    def outer_copy(k):
        number, device = outer_device(k)
        return pltpu.make_async_remote_copy(
            src_ref=z_in.at[rows_of(my_outer)],
            dst_ref=z_in.at[rows_of(my_outer)],
            send_sem=ar_send.at[1],
            recv_sem=ar_recv.at[1],
            device_id=device,
            device_id_type=MESH,
        )

    def gather_copy(k):
        number, device = inner_device(k)
        return pltpu.make_async_remote_copy(
            src_ref=ar_out.at[rows_of(my_inner)],
            dst_ref=ar_out.at[rows_of(my_inner)],
            send_sem=ar_send.at[2],
            recv_sem=ar_recv.at[2],
            device_id=device,
            device_id_type=MESH,
        )

    def start_many(copy_of, number):
        def step(k, carry):
            copy_of(k).start()
            return carry

        lax.fori_loop(1, number, step, 0)

    def wait_many(buffer, number, sem):
        part = buffer.at[0 : (number - 1) * chunk]
        pltpu.make_async_copy(part, part, sem).wait()

    start_many(scatter_copy, inner)
    place(0, conj_times(probe, entry_grad))
    send_all(lambda d: fold_copy(0, d))

    ar_in[rows_of(my_inner)] = ar_src[rows_of(my_inner)]
    wait_many(ar_in, inner, ar_recv.at[0])
    z_in[rows_of(my_outer)] = sum(ar_in[k * chunk : (k + 1) * chunk] for k in range(inner))
    start_many(outer_copy, outer)

    receive_all(lambda d: fold_copy(1, d))
    finish(1)

    wait_many(z_in, outer, ar_recv.at[1])
    positions = count * n_row * n_col
    ar_out[rows_of(my_inner)] = sum(z_in[k * chunk : (k + 1) * chunk] for k in range(outer)) * (
        1.0 / math.sqrt(positions)
    )
    start_many(gather_copy, inner)

    receive_all(lambda d: fold_copy(0, d))
    finish(0)

    wait_many(ar_out, inner, ar_recv.at[2])
    probe_copies = [
        pltpu.make_async_copy(
            ar_out.at[part * side : (part + 1) * side], pg_ref.at[part], local_sem.at[2 + part]
        )
        for part in range(2)
    ]
    for copy in probe_copies:
        copy.start()
    wait_many(ar_src, inner, ar_send.at[0])
    wait_many(z_in, outer, ar_send.at[1])
    wait_many(ar_out, inner, ar_send.at[2])
    for s in range(2):
        sent_all(lambda d: halo_copy(s, d))
        sent_all(lambda d: fold_copy(s, d))
        out_copy(s).wait()
    for copy in probe_copies:
        copy.wait()


def on_device(mesh_shape, table, fresnel, objects, illumination, intensity, row_offset, col_offset):
    n_row, n_col = mesh_shape
    outer = (n_row // plane_rows) * (n_col // plane_cols)
    chunk = 2 * side // (plane_rows * plane_cols)
    scratch = [
        (4, 2, 2 * side, side),
        (4, 2, 2 * side, side),
        (2, side, side),
        (2, side, side),
        (2, 2 * side, side),
        (2, 2 * side, side),
        (2, side, side),
        (count, side, side),
        None,
        (2, side, side),
        (count * side, 2 * side),
        (count * side, 2 * side),
        (count * side, 2 * side),
        (2, 2 * side, 3 * side),
        (2, 2 * side, 3 * side),
        (2, 2 * side, side),
        (2, 2 * side, side),
        (2, 2, 2, half, tile_w),
        (2, 2 * side, side),
        (2, 2 * side, side),
        (2, 2, side, tile_w),
        (2 * side, side),
        (2 * side, side),
        (outer * chunk, side),
        (2 * side, side),
    ]
    scratch = [
        pltpu.VMEM((4, 2 * side, 2 * side), bf16) if shape is None else pltpu.VMEM(shape, f32)
        for shape in scratch
    ]
    dma = pltpu.SemaphoreType.DMA
    scratch += [dma((8,)), dma((2, 8)), dma((2, 8)), dma((2, 8)), dma((2, 8)), dma((3,)), dma((3,))]
    smem = pl.BlockSpec(memory_space=pltpu.SMEM)
    anywhere = pl.BlockSpec(memory_space=pl.ANY)
    return pl.pallas_call(
        functools.partial(kernel, mesh_shape),
        out_shape=(
            jax.ShapeDtypeStruct(objects.shape, f32),
            jax.ShapeDtypeStruct(illumination.shape, f32),
        ),
        in_specs=[smem, smem] + [anywhere] * 5,
        out_specs=(anywhere, anywhere),
        scratch_shapes=scratch,
        compiler_params=pltpu.CompilerParams(
            collective_id=0, has_side_effects=True, vmem_limit_bytes=48 * 1024 * 1024
        ),
        name="ptychography",
    )(row_offset, col_offset, objects, illumination, intensity, table, fresnel)


def solution(mesh):
    table, fresnel = tables()
    shape = (mesh.shape["row"], mesh.shape["col"])

    def whole(objects, illumination, intensity, row_offset, col_offset):
        return jax.shard_map(
            functools.partial(on_device, shape),
            mesh=mesh,
            in_specs=(
                P(),
                P(),
                P(None, None, "row", "col"),
                P(),
                P(("row", "col"), None, None),
                P(("row", "col")),
                P(("row", "col")),
            ),
            out_specs=(P(None, None, "row", "col"), P()),
            check_vma=False,
        )(jnp.asarray(table), jnp.asarray(fresnel), objects, illumination, intensity, row_offset, col_offset)

    return whole
```

time: 612 us -> 88.5 us (0.14)
  waiting for transfers between devices: 481 us -> 0 us
  Pallas kernels: 0 us -> 79.9 us
  local copies, waits for them, and re-layouts: 40.4 us -> 7.59 us
  starting transfers between devices: 25.8 us -> 0 us
  matrix products: 24 us -> 0 us
  loops' own time: 16.1 us -> 0 us
  between operations: 14.6 us -> 0.65 us
  other arithmetic: 9.12 us -> 0 us
    psum x1 -> x0, waiting for transfers between devices: 455 us -> none  [on_device(): probe_total = lax.psum(probe_local, ('row', 'col'))]
    pallas_call x0 -> x1, Pallas kernels: none -> 79.9 us  [on_device(): pl.pallas_call(functools.partial(kernel, mesh_shape), out_shape=(jax.Shap...]
    ppermute x8 -> x0, starting transfers between devices: 25.8 us -> none  [the longest x4 15.8 us: extended(): lax.ppermute(lax.slice_in_dim(block, block.shape[dim] - width, None, axis...]
    ppermute x8 -> x0, waiting for transfers between devices: 25.6 us -> none  [the longest x4 16.1 us: extended(): lax.ppermute(lax.slice_in_dim(block, 0, width, axis=dim), axis, backward)]
    dot_general x24 -> x0, matrix products: 24 us -> none  [the longest x6 6.24 us: spectrum(): with_sin = jnp.einsum('ij,...jk->...ik', sine, middle, precision=highest)]
    another operation x3 -> x0, loops' own time: 16.1 us -> none  [the longest x1 15.7 us: on_device(): lax.fori_loop(0, count, place, jnp.zeros((2, 2, padded_height, padded_wid...]
    gather x24 -> x0, local copies, waits for them, and re-layouts: 16 us -> none
    dynamic_update_slice x4 -> x0, local copies, waits for them, and re-layouts: 12.4 us -> none  [place(): return lax.dynamic_update_slice(running, previous + stacked[number], corner)]
  transfers between devices with their start and end apart: 9 -> 0, of which waited for: 7 -> 0; matrix products, arithmetic and copies ran while one was open for 1% -> 0% of each run, Pallas kernels for 0% -> 0%
where the time goes in v1:
time: 88.5 us; the launch traced here: 88.2 us
  Pallas kernels  79.9 us (90%)
  local copies, waits for them, and re-layouts  7.59 us (9%)
    pallas_call x1, Pallas kernels, on_device(): pl.pallas_call(functools.partial(kernel, mesh_shape), out_shape=(jax.Shap...  79.9 us
    unnamed x16, local copies, waits for them, and re-layouts  7.59 us

profile of v1, /device:TPU:1, one launch (start us, length us, event | category | flops | bytes accessed | tf_op | source)
XLA Modules:
  0.0 88.2 jit_solution(11160395134795297399)
XLA Ops:
  0.6 0.0 copy-start
  0.6 1.0 %copy-done = f32[2,2,128,256]{3,2,1,0:T(8,128)S(1)} copy-done((f32[2,2,128,256]{3,2,1,0:T(8,128)S(1)}, f32[2,2,128,256]{3,2,1,0:T(8,128)}, u32[]{:S(2)}) %copy-start) | copy-done | bytes 524312
  1.7 0.0 copy-start.1
  1.7 1.0 %copy-done.1 = bf16[4,256,256]{2,1,0:T(8,128)(2,1)S(1)} copy-done((bf16[4,256,256]{2,1,0:T(8,128)(2,1)S(1)}, bf16[4,256,256]{2,1,0:T(8,128)(2,1)}, u32[]{:S(2)}) %copy-start.1) | copy-done | bytes 524312
  2.7 0.0 copy-start.2
  2.7 0.9 %copy-done.2 = f32[4,128,128]{2,1,0:T(8,128)S(1)} copy-done((f32[4,128,128]{2,1,0:T(8,128)S(1)}, f32[4,128,128]{2,1,0:T(8,128)}, u32[]{:S(2)}) %copy-start.2) | copy-done | bytes 262168
  3.7 0.0 copy-start.3
  3.7 0.9 %copy-done.3 = f32[2,128,128]{2,1,0:T(8,128)S(1)} copy-done((f32[2,128,128]{2,1,0:T(8,128)S(1)}, f32[2,128,128]{2,1,0:T(8,128)}, u32[]{:S(2)}) %copy-start.3) | copy-done | bytes 131096
  4.6 0.0 copy-start.4
  4.6 0.9 %copy-done.4 = f32[2,128,128]{2,1,0:T(8,128)S(1)} copy-done((f32[2,128,128]{2,1,0:T(8,128)S(1)}, f32[2,128,128]{2,1,0:T(8,128)}, u32[]{:S(2)}) %copy-start.4) | copy-done | bytes 131096
  5.5 0.0 copy-start.5
  5.5 0.7 copy-done.5
  6.1 0.0 copy-start.6
  6.1 0.7 copy-done.6
  6.8 79.9 %ptychography.1 = (f32[2,2,128,256]{3,2,1,0:T(8,128)S(1)}, f32[2,128,128]{2,1,0:T(8,128)S(1)}) custom-call(s32[4]{0:T(128)S(1)} %copy-done.5, s32[4]{0:T(128)S(1)} %copy-done.6, f32[2,2,128,256]{3,2,1,0:T(8,128)S(1)} %copy-done, f32[2,128,128]{2,1,0:T(8,128)S(1)} %copy-done.3, f32[4,128,128]{2,1,0:T(8,128)S(1)} %copy-done.2, ...), custom_call_target="tpu_custom_call" | custom-call | tf_op jit(solution)/shard_map/ptychography/pallas_call | solution.py:598
  86.7 0.8 copy.11
  87.5 0.7 copy.12
Async XLA Ops:
  0.6 1.0 %copy-start = (f32[2,2,128,256]{3,2,1,0:T(8,128)S(1)}, f32[2,2,128,256]{3,2,1,0:T(8,128)}, u32[]{:S(2)}) copy-start(f32[2,2,128,256]{3,2,1,0:T(8,128)} %obj_ref.1) | copy-start | bytes 1572868
  1.7 1.0 %copy-start.1 = (bf16[4,256,256]{2,1,0:T(8,128)(2,1)S(1)}, bf16[4,256,256]{2,1,0:T(8,128)(2,1)}, u32[]{:S(2)}) copy-start(bf16[4,256,256]{2,1,0:T(8,128)(2,1)} %constant.4.clone.tab_ref) | copy-start | bytes 1572868
  2.7 0.9 %copy-start.2 = (f32[4,128,128]{2,1,0:T(8,128)S(1)}, f32[4,128,128]{2,1,0:T(8,128)}, u32[]{:S(2)}) copy-start(f32[4,128,128]{2,1,0:T(8,128)} %int_ref.1) | copy-start | bytes 786436
  3.7 0.9 %copy-start.3 = (f32[2,128,128]{2,1,0:T(8,128)S(1)}, f32[2,128,128]{2,1,0:T(8,128)}, u32[]{:S(2)}) copy-start(f32[2,128,128]{2,1,0:T(8,128)} %ill_ref.1) | copy-start | bytes 393220
  4.6 0.9 %copy-start.4 = (f32[2,128,128]{2,1,0:T(8,128)S(1)}, f32[2,128,128]{2,1,0:T(8,128)}, u32[]{:S(2)}) copy-start(f32[2,128,128]{2,1,0:T(8,128)} %constant.5.clone.fres_ref) | copy-start | bytes 393220
  5.5 0.7 copy-start.5
  6.1 0.7 copy-start.6

commit v2 on v1

--- a/solution.py
+++ b/solution.py
@@ -16,6 +16,8 @@
 tile_w = 256
 count = 4
 plane_rows = 8
+direct = 40
+rest = half - direct
 plane_cols = 4
 directions = ((-1, 0), (1, 0), (0, -1), (0, 1), (-1, -1), (-1, 1), (1, -1), (1, 1))
 MESH = pl.DeviceIdType.MESH
@@ -87,11 +89,13 @@
     ar_in,
     z_in,
     ar_out,
+    relay_corner,
+    relay_rest,
     local_sem,
-    halo_send,
-    halo_recv,
-    fold_send,
-    fold_recv,
+    msg_send,
+    msg_recv,
+    relay_send,
+    relay_recv,
     ar_send,
     ar_recv,
 ):
@@ -119,6 +123,46 @@
     for copy in own[0] + own[1] + loads:
         copy.start()
 
+    messages = [(d, 0, half if d[1] else direct) for d in directions]
+    messages += [((-1, 0), direct, rest), ((1, 0), direct, rest)]
+
+    def halo_dst(s, m):
+        (dr, dc), first, size = messages[m]
+        if dc == 0:
+            start = first + (3 * half if dr < 0 else 0)
+            return pads[s].at[1:3, :, start : start + size]
+        into = west_in if dc > 0 else east_in
+        start, size = ((half, side) if dr == 0 else (3 * half, half) if dr < 0 else (0, half))
+        return into.at[s, start : start + size]
+
+    def halo_src(s, m):
+        (dr, dc), first, size = messages[m]
+        if dc == 0:
+            start = first + (half if dr < 0 else side)
+            return pads[s].at[1:3, :, start : start + size]
+        start, size = ((0, side) if dr == 0 else (0, half) if dr < 0 else (half, half))
+        return (east_src if dc > 0 else west_src).at[s, start : start + size]
+
+    def fold_dst(s, m):
+        (dr, dc), first, size = messages[m]
+        if dc == 0:
+            return ns_in.at[s, 1 if dr < 0 else 0, :, :, first : first + size]
+        into = fw_in if dc > 0 else fe_in
+        start, size = ((0, side) if dr == 0 else (3 * half, half) if dr < 0 else (side, half))
+        return into.at[s, start : start + size]
+
+    def fold_src(s, m):
+        (dr, dc), first, size = messages[m]
+        if dc == 0:
+            start = first + (0 if dr < 0 else 3 * half)
+            return accs[s].at[0:2, :, start : start + size]
+        start, size = ((half, side) if dr == 0 else (0, half) if dr < 0 else (3 * half, half))
+        return (fe_src if dc > 0 else fw_src).at[s, start : start + size]
+
+    ends = ((halo_src, halo_dst), (fold_src, fold_dst))
+    row_in, row_out = lax.rem(row, plane_rows), lax.div(row, plane_rows)
+    n_out = n_row // plane_rows
+
     def has(dr, dc):
         found = None
         if dr:
@@ -128,65 +172,96 @@
             found = col_found if found is None else jnp.logical_and(found, col_found)
         return found
 
-    def halo_dst(s, dr, dc):
-        if dc == 0:
-            start = 3 * half if dr < 0 else 0
-            return pads[s].at[1:3, :, start : start + half]
-        into = west_in if dc > 0 else east_in
-        start, size = ((half, side) if dr == 0 else (3 * half, half) if dr < 0 else (0, half))
-        return into.at[s, start : start + size]
-
-    def halo_copy(s, d):
-        dr, dc = directions[d]
-        if dc == 0:
-            start = half if dr < 0 else side
-            src = pads[s].at[1:3, :, start : start + half]
-        else:
-            start, size = ((0, side) if dr == 0 else (0, half) if dr < 0 else (half, half))
-            src = (east_src if dc > 0 else west_src).at[s, start : start + size]
+    def also(*flags):
+        return functools.reduce(jnp.logical_and, [flag for flag in flags if flag is not None])
+
+    def relayed(m):
+        (dr, dc), first, _ = messages[m]
+        return dr != 0 and (dc != 0 or first != 0)
+
+    def relay_at(m):
+        (dr, dc), _, _ = messages[m]
+        number = 2 if dc == 0 else 1 if dc > 0 else 0
+        return 2 * number + (1 if dr > 0 else 2)
+
+    def sends(m):
+        return has(*messages[m][0])
+
+    def receives(m):
+        dr, dc = messages[m][0]
+        return has(-dr, -dc)
+
+    def leaves_group(m):
+        return row_in == (plane_rows - 1 if messages[m][0][0] > 0 else 0)
+
+    def enters_group(m):
+        return row_in == (0 if messages[m][0][0] > 0 else plane_rows - 1)
+
+    def relays(m):
+        dr, dc = messages[m][0]
+        group = (row_out > 0) if dr < 0 else (row_out < n_out - 1)
+        return also(row_in == relay_at(m), group, has(0, dc) if dc else None)
+
+    def relay_row(m):
+        dr = messages[m][0][0]
+        return row + 1 - plane_rows + relay_at(m) if dr > 0 else row + relay_at(m)
+
+    def target_of_relay(m):
+        dr, dc = messages[m][0]
+        return row - relay_at(m) + (plane_rows if dr > 0 else -1), col + dc
+
+    def relay_buffer(phase, s, m):
+        return (relay_rest if messages[m][0][1] == 0 else relay_corner).at[phase, s]
+
+    def remote(src, dst, send, recv, device):
         return pltpu.make_async_remote_copy(
             src_ref=src,
-            dst_ref=halo_dst(s, dr, dc),
-            send_sem=halo_send.at[s, d],
-            recv_sem=halo_recv.at[s, d],
-            device_id=(row + dr, col + dc),
+            dst_ref=dst,
+            send_sem=send,
+            recv_sem=recv,
+            device_id=device,
             device_id_type=MESH,
         )
 
-    def fold_dst(s, dr, dc):
-        if dc == 0:
-            return ns_in.at[s, 1 if dr < 0 else 0]
-        into = fw_in if dc > 0 else fe_in
-        start, size = ((0, side) if dr == 0 else (3 * half, half) if dr < 0 else (side, half))
-        return into.at[s, start : start + size]
-
-    def fold_copy(s, d):
-        dr, dc = directions[d]
-        start, size = ((half, side) if dr == 0 else (0, half) if dr < 0 else (3 * half, half))
-        if dc == 0:
-            src = accs[s].at[:, start : start + size, 0:tile_w]
-        else:
-            src = (fe_src if dc > 0 else fw_src).at[s, start : start + size]
-        return pltpu.make_async_remote_copy(
-            src_ref=src,
-            dst_ref=fold_dst(s, dr, dc),
-            send_sem=fold_send.at[s, d],
-            recv_sem=fold_recv.at[s, d],
-            device_id=(row + dr, col + dc),
-            device_id_type=MESH,
-        )
-
-    for dr, dc in directions:
-
-        @pl.when(jnp.logical_not(has(-dr, -dc)))
-        def _(dr=dr, dc=dc):
+    def straight(phase, s, m):
+        src, dst = ends[phase]
+        dr, dc = messages[m][0]
+        return remote(
+            src(s, m),
+            dst(s, m),
+            msg_send.at[phase, s, m],
+            msg_recv.at[phase, s, m],
+            (row + dr, col + dc),
+        )
+
+    def to_relay(phase, s, m):
+        return remote(
+            ends[phase][0](s, m),
+            relay_buffer(phase, s, m),
+            msg_send.at[phase, s, m],
+            relay_recv.at[phase, s],
+            (relay_row(m), col),
+        )
+
+    def from_relay(phase, s, m):
+        return remote(
+            relay_buffer(phase, s, m),
+            ends[phase][1](s, m),
+            relay_send.at[phase, s],
+            msg_recv.at[phase, s, m],
+            target_of_relay(m),
+        )
+
+    for m in range(len(messages)):
+
+        @pl.when(jnp.logical_not(receives(m)))
+        def _(m=m):
             for s in range(2):
-                for dst in (halo_dst(s, dr, dc), fold_dst(s, dr, dc)):
+                for dst in (halo_dst(s, m), fold_dst(s, m)):
                     dst[...] = jnp.zeros(dst.shape, f32)
 
     inner, outer = plane_rows * plane_cols, (n_row // plane_rows) * (n_col // plane_cols)
     outer_cols = n_col // plane_cols
-    row_in, row_out = lax.rem(row, plane_rows), lax.div(row, plane_rows)
     col_in, col_out = lax.rem(col, plane_cols), lax.div(col, plane_cols)
     my_inner = row_in * plane_cols + col_in
     my_outer = row_out * outer_cols + col_out
@@ -207,15 +282,30 @@
 
     barrier = pltpu.get_barrier_semaphore()
     expected = jnp.int32(inner + outer - 2)
-    for dr, dc in directions:
-        found = has(dr, dc)
-        expected = expected + found.astype(jnp.int32)
-
-        @pl.when(found)
-        def _(dr=dr, dc=dc):
-            pl.semaphore_signal(
-                barrier, inc=1, device_id=(row + dr, col + dc), device_id_type=MESH
+
+    def greet_if(flag, device):
+        @pl.when(flag)
+        def _():
+            pl.semaphore_signal(barrier, inc=1, device_id=device, device_id_type=MESH)
+
+    for m in range(len(messages)):
+        dr, dc = messages[m][0]
+        expected = expected + sends(m).astype(jnp.int32)
+        if relayed(m):
+            expected = expected + relays(m).astype(jnp.int32)
+            greet_if(
+                also(receives(m), jnp.logical_not(enters_group(m))), (row - dr, col - dc)
             )
+            greet_if(
+                also(receives(m), enters_group(m)),
+                (row + relay_at(m) + (-plane_rows if dr > 0 else 1), col - dc),
+            )
+            greet_if(
+                relays(m),
+                (row - relay_at(m) + (plane_rows - 1 if dr > 0 else 0), col),
+            )
+        else:
+            greet_if(receives(m), (row - dr, col - dc))
 
     def greet(device_of):
         def step(k, carry):
@@ -227,27 +317,49 @@
     lax.fori_loop(1, inner, greet(inner_device), 0)
     lax.fori_loop(1, outer, greet(outer_device), 0)
 
-    def send_all(copy_of):
-        for d in range(8):
-
-            @pl.when(has(*directions[d]))
-            def _(d=d):
-                copy_of(d).start()
-
-    def receive_all(copy_of):
-        for d in range(8):
-            dr, dc = directions[d]
-
-            @pl.when(has(-dr, -dc))
-            def _(d=d):
-                copy_of(d).wait_recv()
-
-    def sent_all(copy_of):
-        for d in range(8):
-
-            @pl.when(has(*directions[d]))
-            def _(d=d):
-                copy_of(d).wait_send()
+    def each(phase, s, straight_do, relay_do=None):
+        for m in range(len(messages)):
+            if relayed(m):
+                flag = also(sends(m), jnp.logical_not(leaves_group(m)))
+
+                @pl.when(also(sends(m), leaves_group(m)))
+                def _(m=m):
+                    straight_do(to_relay(phase, s, m))
+
+            else:
+                flag = sends(m)
+
+            @pl.when(flag)
+            def _(m=m):
+                straight_do(straight(phase, s, m))
+
+            if relay_do is not None and relayed(m):
+
+                @pl.when(relays(m))
+                def _(m=m):
+                    relay_do(from_relay(phase, s, m))
+
+    def send_all(phase, s):
+        each(phase, s, lambda copy: copy.start())
+
+    def pass_on(phase, s):
+        for m in range(len(messages)):
+            if relayed(m):
+
+                @pl.when(relays(m))
+                def _(m=m):
+                    to_relay(phase, s, m).wait_recv()
+                    from_relay(phase, s, m).start()
+
+    def receive_all(phase, s):
+        for m in range(len(messages)):
+
+            @pl.when(receives(m))
+            def _(m=m):
+                straight(phase, s, m).wait_recv()
+
+    def sent_all(phase, s):
+        each(phase, s, lambda copy: copy.wait_send(), lambda copy: copy.wait_send())
 
     lane = lax.broadcasted_iota(jnp.int32, (1, side), 1)
     lower = lane < half
@@ -265,9 +377,9 @@
 
     pack_edges(0)
     pl.semaphore_wait(barrier, expected)
-    send_all(lambda d: halo_copy(0, d))
+    send_all(0, 0)
     pack_edges(1)
-    send_all(lambda d: halo_copy(1, d))
+    send_all(0, 1)
 
     row_at = [row_ref[j] for j in range(count)]
     col_at = [col_ref[j] for j in range(count)]
@@ -404,8 +516,10 @@
             )
             part_sum = dot(place_rows, both)
             total = part_sum if total is None else total + part_sum
-        accs[s][0] = total[:, : 3 * side]
-        accs[s][1] = total[:, 3 * side :]
+        for part in range(2):
+            for tile in range(3):
+                start = (3 * part + tile) * side
+                accs[s][tile, part] = total[:, start : start + side]
         halo_real, halo_imag = total[:, 2 * side : 3 * side], total[:, 5 * side :]
         turned = pltpu.roll(halo_imag, half, 1)
         fe_src[s] = jnp.where(lower, halo_real, turned)
@@ -419,17 +533,14 @@
                 from_west = pltpu.roll(from_west, half, 1)
                 from_east = pltpu.roll(from_east, half, 1)
             rows = slice(half, half + side)
-            above_below = jnp.concatenate([ns_in[s, 0, part], ns_in[s, 1, part]], axis=0)
-            og[s, part, :, 0:side] = (
-                accs[s][part, rows, 0:side]
-                + above_below[:, 0:side]
-                + jnp.where(lower, from_west, 0.0)
-            )
-            og[s, part, :, side:tile_w] = (
-                accs[s][part, rows, side:tile_w]
-                + above_below[:, side:tile_w]
-                + jnp.where(lower, 0.0, from_east)
-            )
+            for tile in range(2):
+                beside = jnp.where(lower == (tile == 0), from_east if tile else from_west, 0.0)
+                above_below = jnp.concatenate(
+                    [ns_in[s, 0, tile, part], ns_in[s, 1, tile, part]], axis=0
+                )
+                og[s, part, :, tile * side : (tile + 1) * side] = (
+                    accs[s][tile, part, rows] + above_below + beside
+                )
         out_copy(s).start()
 
     def out_copy(s):
@@ -440,12 +551,14 @@
     illumination = jnp.concatenate([ill[0], ill[1]], axis=1)
     probe = jnp.concatenate([illumination] * count, axis=0)
 
-    receive_all(lambda d: halo_copy(0, d))
+    pass_on(0, 0)
+    receive_all(0, 0)
     join_halo(0)
     gather(0, first_w)
+    pass_on(0, 1)
     moved_s[...] = propagate(times(probe, first_w[...]), 1.0)
 
-    receive_all(lambda d: halo_copy(1, d))
+    receive_all(0, 1)
     join_halo(1)
     gather(1, second_w)
     far = by_cols(stand(by_rows(times(moved_s[...], second_w[...]))))
@@ -457,7 +570,7 @@
     exit_grad = by_rows(lie(by_cols(far_grad, True)), True)
 
     place(1, conj_times(moved_s[...], exit_grad))
-    send_all(lambda d: fold_copy(1, d))
+    send_all(1, 1)
 
     entry_grad = propagate(conj_times(second_w[...], exit_grad), -1.0)
     probe_local = conj_times(first_w[...], entry_grad)
@@ -511,19 +624,22 @@
         lax.fori_loop(1, number, step, 0)
 
     def wait_many(buffer, number, sem):
+        if number == 1:
+            return
         part = buffer.at[0 : (number - 1) * chunk]
         pltpu.make_async_copy(part, part, sem).wait()
 
     start_many(scatter_copy, inner)
     place(0, conj_times(probe, entry_grad))
-    send_all(lambda d: fold_copy(0, d))
+    send_all(1, 0)
 
     ar_in[rows_of(my_inner)] = ar_src[rows_of(my_inner)]
     wait_many(ar_in, inner, ar_recv.at[0])
     z_in[rows_of(my_outer)] = sum(ar_in[k * chunk : (k + 1) * chunk] for k in range(inner))
     start_many(outer_copy, outer)
 
-    receive_all(lambda d: fold_copy(1, d))
+    pass_on(1, 1)
+    receive_all(1, 1)
     finish(1)
 
     wait_many(z_in, outer, ar_recv.at[1])
@@ -533,7 +649,8 @@
     )
     start_many(gather_copy, inner)
 
-    receive_all(lambda d: fold_copy(0, d))
+    pass_on(1, 0)
+    receive_all(1, 0)
     finish(0)
 
     wait_many(ar_out, inner, ar_recv.at[2])
@@ -549,8 +666,8 @@
     wait_many(z_in, outer, ar_send.at[1])
     wait_many(ar_out, inner, ar_send.at[2])
     for s in range(2):
-        sent_all(lambda d: halo_copy(s, d))
-        sent_all(lambda d: fold_copy(s, d))
+        sent_all(0, s)
+        sent_all(1, s)
         out_copy(s).wait()
     for copy in probe_copies:
         copy.wait()
@@ -574,11 +691,11 @@
         (count * side, 2 * side),
         (count * side, 2 * side),
         (count * side, 2 * side),
-        (2, 2 * side, 3 * side),
-        (2, 2 * side, 3 * side),
+        (3, 2, 2 * side, side),
+        (3, 2, 2 * side, side),
         (2, 2 * side, side),
         (2, 2 * side, side),
-        (2, 2, 2, half, tile_w),
+        (2, 2, 2, 2, half, side),
         (2, 2 * side, side),
         (2, 2 * side, side),
         (2, 2, side, tile_w),
@@ -586,15 +703,17 @@
         (2 * side, side),
         (outer * chunk, side),
         (2 * side, side),
+        (2, 2, half, side),
+        (2, 2, 2, 2, rest, side),
     ]
     scratch = [
         pltpu.VMEM((4, 2 * side, 2 * side), bf16) if shape is None else pltpu.VMEM(shape, f32)
         for shape in scratch
     ]
     dma = pltpu.SemaphoreType.DMA
-    scratch += [dma((8,)), dma((2, 8)), dma((2, 8)), dma((2, 8)), dma((2, 8)), dma((3,)), dma((3,))]
+    scratch += [dma((8,)), dma((2, 2, 10)), dma((2, 2, 10)), dma((2, 2)), dma((2, 2)), dma((3,)), dma((3,))]
     smem = pl.BlockSpec(memory_space=pltpu.SMEM)
-    anywhere = pl.BlockSpec(memory_space=pl.ANY)
+    anywhere = pl.BlockSpec(memory_space=pltpu.HBM)
     return pl.pallas_call(
         functools.partial(kernel, mesh_shape),
         out_shape=(
@@ -605,7 +724,7 @@
         out_specs=(anywhere, anywhere),
         scratch_shapes=scratch,
         compiler_params=pltpu.CompilerParams(
-            collective_id=0, has_side_effects=True, vmem_limit_bytes=48 * 1024 * 1024
+            collective_id=0, has_side_effects=True, vmem_limit_bytes=60 * 1024 * 1024
         ),
         name="ptychography",
     )(row_offset, col_offset, objects, illumination, intensity, table, fresnel)

time: 88.5 us -> 63.2 us (0.71)
  Pallas kernels: 79.9 us -> 59.8 us
  local copies, waits for them, and re-layouts: 7.59 us -> 2.56 us
    pallas_call x1, Pallas kernels: 79.9 us -> 59.8 us  [on_device(): pl.pallas_call(functools.partial(kernel, mesh_shape), out_shape=(jax.Shap...]
    unnamed x16 -> x4, local copies, waits for them, and re-layouts: 7.59 us -> 2.56 us
where the time goes in v2:
time: 63.2 us; the launch traced here: 63.1 us
  Pallas kernels  59.8 us (95%)
  local copies, waits for them, and re-layouts  2.56 us (4%)
  between operations  0.65 us (1%)
    pallas_call x1, Pallas kernels, on_device(): pl.pallas_call(functools.partial(kernel, mesh_shape), out_shape=(jax.Shap...  59.8 us
    unnamed x4, local copies, waits for them, and re-layouts  2.56 us

profile of v2, /device:TPU:1, one launch (start us, length us, event | category | flops | bytes accessed | tf_op | source)
XLA Modules:
  0.0 63.1 jit_solution(15509161221697037264)
XLA Ops:
  0.6 59.8 %ptychography.1 = (f32[2,2,128,256]{3,2,1,0:T(8,128)}, f32[2,128,128]{2,1,0:T(8,128)}) custom-call(s32[4]{0:T(128)} %row_ref.1, s32[4]{0:T(128)} %col_ref.1, f32[2,2,128,256]{3,2,1,0:T(8,128)} %obj_ref.1, f32[2,128,128]{2,1,0:T(8,128)} %ill_ref.1, f32[4,128,128]{2,1,0:T(8,128)} %int_ref.1, bf16[4,256,256]{2,1,0:T(8,128)(2,1)} %constant.4.clone.tab_ref, ...), custom_call_target="tpu_custom_call" | custom-call | tf_op jit(solution)/shard_map/ptychography/pallas_call | solution.py:717
  60.5 0.0 copy-start
  60.5 1.9 %copy.11 = f32[2,2,128,256]{3,2,1,0:T(8,128)} copy(f32[2,2,128,256]{3,2,1,0:T(8,128)} %get-tuple-element.4) | data formatting | bytes 1048576
  62.4 0.0 copy-done
  62.4 0.7 %copy.12 = f32[2,128,128]{2,1,0:T(8,128)} copy(f32[2,128,128]{2,1,0:T(8,128)S(1)} %copy-done) | data formatting | bytes 262144
Async XLA Ops:
  60.5 1.9 %copy-start = (f32[2,128,128]{2,1,0:T(8,128)S(1)}, f32[2,128,128]{2,1,0:T(8,128)}, u32[]{:S(2)}) copy-start(f32[2,128,128]{2,1,0:T(8,128)} %get-tuple-element.5) | copy-start | bytes 393220

commit v3 on v2

--- a/solution.py
+++ b/solution.py
@@ -98,6 +98,7 @@
     relay_recv,
     ar_send,
     ar_recv,
+    stage_sem,
 ):
     n_row, n_col = mesh_shape
     row, col = lax.axis_index("row"), lax.axis_index("col")
@@ -266,28 +267,58 @@
     my_inner = row_in * plane_cols + col_in
     my_outer = row_out * outer_cols + col_out
 
-    def inner_device(k):
-        number = lax.rem(my_inner + k, inner)
-        return number, (
-            row_out * plane_rows + lax.div(number, plane_cols),
-            col_out * plane_cols + lax.rem(number, plane_cols),
-        )
-
-    def outer_device(k):
-        number = lax.rem(my_outer + k, outer)
+    def hops(step, size):
+        return min(step, size - step)
+
+    core_rows = plane_rows // 2
+    inner_steps = [
+        (y, core, x) for y in range(core_rows) for core in range(2) for x in range(plane_cols)
+    ]
+    inner_steps.sort(key=lambda k: -2 * (hops(k[0], core_rows) + hops(k[2], plane_cols)) - k[1])
+    outer_steps = sorted(range(1, outer), key=lambda k: -hops(k, outer))
+
+    def inner_device(step):
+        y, core, x = step
+        row_to = lax.rem(lax.div(row_in, 2) + y, core_rows) * 2 + lax.rem(row_in + core, 2)
+        col_to = lax.rem(col_in + x, plane_cols)
+        number = row_to * plane_cols + col_to
+        return number, (row_out * plane_rows + row_to, col_out * plane_cols + col_to)
+
+    def outer_device(step):
+        number = lax.rem(my_outer + step, outer)
         return number, (
             lax.div(number, outer_cols) * plane_rows + row_in,
             lax.rem(number, outer_cols) * plane_cols + col_in,
         )
 
     barrier = pltpu.get_barrier_semaphore()
-    expected = jnp.int32(inner + outer - 2)
+    expected = jnp.int32(0)
 
     def greet_if(flag, device):
         @pl.when(flag)
         def _():
             pl.semaphore_signal(barrier, inc=1, device_id=device, device_id_type=MESH)
 
+    def greet(devices, semaphore):
+        for device in devices:
+            pl.semaphore_signal(semaphore, inc=1, device_id=device, device_id_type=MESH)
+
+    def turn(index, step, size):
+        return index - lax.rem(index, size) + lax.rem(lax.rem(index, size) + step, size)
+
+    def far_row(step):
+        return lax.rem(row + step * plane_rows, n_row), col
+
+    def far_col(step):
+        return row, lax.rem(col + step * plane_cols, n_col)
+
+    line_far = [far_row(k) for k in sorted({1 % n_out, (n_out - 1) % n_out} - {0})]
+    line_near = [far_col(k) for k in range(1, outer_cols)]
+    line_x = [(row, turn(col, k, plane_cols)) for k in range(1, plane_cols)]
+    line_y = [(turn(row, k, plane_rows), col) for k in range(1, plane_rows)]
+    lines = line_far + line_near + line_y + line_x
+    expected = expected + len(lines)
+    greet(line_far, barrier)
     for m in range(len(messages)):
         dr, dc = messages[m][0]
         expected = expected + sends(m).astype(jnp.int32)
@@ -306,19 +337,22 @@
             )
         else:
             greet_if(receives(m), (row - dr, col - dc))
-
-    def greet(device_of):
-        def step(k, carry):
-            pl.semaphore_signal(barrier, inc=1, device_id=device_of(k)[1], device_id_type=MESH)
-            return carry
-
-        return step
-
-    lax.fori_loop(1, inner, greet(inner_device), 0)
-    lax.fori_loop(1, outer, greet(outer_device), 0)
+    greet(line_near + line_y + line_x, barrier)
+
+    def second_stage():
+        greet(line_far + line_x, stage_sem.at[0])
+
+    def third_stage():
+        pl.semaphore_wait(stage_sem.at[0], len(line_far + line_x))
+        greet(line_near, stage_sem.at[1])
+
+    def last_stage():
+        pl.semaphore_wait(stage_sem.at[1], len(line_near))
+
+    order = sorted(range(len(messages)), key=lambda m: not relayed(m))
 
     def each(phase, s, straight_do, relay_do=None):
-        for m in range(len(messages)):
+        for m in order:
             if relayed(m):
                 flag = also(sends(m), jnp.logical_not(leaves_group(m)))
 
@@ -378,6 +412,7 @@
     pack_edges(0)
     pl.semaphore_wait(barrier, expected)
     send_all(0, 0)
+    second_stage()
     pack_edges(1)
     send_all(0, 1)
 
@@ -556,6 +591,7 @@
     join_halo(0)
     gather(0, first_w)
     pass_on(0, 1)
+    third_stage()
     moved_s[...] = propagate(times(probe, first_w[...]), 1.0)
 
     receive_all(0, 1)
@@ -569,8 +605,6 @@
     far_grad = jnp.concatenate([far_real * residual, far_imag * residual], axis=0)
     exit_grad = by_rows(lie(by_cols(far_grad, True)), True)
 
-    place(1, conj_times(moved_s[...], exit_grad))
-    send_all(1, 1)
 
     entry_grad = propagate(conj_times(second_w[...], exit_grad), -1.0)
     probe_local = conj_times(first_w[...], entry_grad)
@@ -616,12 +650,9 @@
             device_id_type=MESH,
         )
 
-    def start_many(copy_of, number):
-        def step(k, carry):
-            copy_of(k).start()
-            return carry
-
-        lax.fori_loop(1, number, step, 0)
+    def start_many(copy_of, steps):
+        for step in steps:
+            copy_of(step).start()
 
     def wait_many(buffer, number, sem):
         if number == 1:
@@ -629,27 +660,30 @@
         part = buffer.at[0 : (number - 1) * chunk]
         pltpu.make_async_copy(part, part, sem).wait()
 
-    start_many(scatter_copy, inner)
+    start_many(scatter_copy, inner_steps[:-1])
+    place(1, conj_times(moved_s[...], exit_grad))
+    send_all(1, 1)
     place(0, conj_times(probe, entry_grad))
     send_all(1, 0)
 
     ar_in[rows_of(my_inner)] = ar_src[rows_of(my_inner)]
+    pass_on(1, 1)
+    pass_on(1, 0)
     wait_many(ar_in, inner, ar_recv.at[0])
     z_in[rows_of(my_outer)] = sum(ar_in[k * chunk : (k + 1) * chunk] for k in range(inner))
-    start_many(outer_copy, outer)
-
-    pass_on(1, 1)
-    receive_all(1, 1)
-    finish(1)
+    last_stage()
+    start_many(outer_copy, outer_steps)
+
 
     wait_many(z_in, outer, ar_recv.at[1])
     positions = count * n_row * n_col
     ar_out[rows_of(my_inner)] = sum(z_in[k * chunk : (k + 1) * chunk] for k in range(outer)) * (
         1.0 / math.sqrt(positions)
     )
-    start_many(gather_copy, inner)
-
-    pass_on(1, 0)
+    start_many(gather_copy, inner_steps[:-1])
+
+    receive_all(1, 1)
+    finish(1)
     receive_all(1, 0)
     finish(0)
 
@@ -671,6 +705,10 @@
         out_copy(s).wait()
     for copy in probe_copies:
         copy.wait()
+
+
+def in_hbm(x):
+    return pltpu.with_memory_space_constraint(x, pltpu.HBM)
 
 
 def on_device(mesh_shape, table, fresnel, objects, illumination, intensity, row_offset, col_offset):
@@ -712,6 +750,7 @@
     ]
     dma = pltpu.SemaphoreType.DMA
     scratch += [dma((8,)), dma((2, 2, 10)), dma((2, 2, 10)), dma((2, 2)), dma((2, 2)), dma((3,)), dma((3,))]
+    scratch += [pltpu.SemaphoreType.REGULAR((2,))]
     smem = pl.BlockSpec(memory_space=pltpu.SMEM)
     anywhere = pl.BlockSpec(memory_space=pltpu.HBM)
     return pl.pallas_call(
@@ -721,13 +760,13 @@
             jax.ShapeDtypeStruct(illumination.shape, f32),
         ),
         in_specs=[smem, smem] + [anywhere] * 5,
-        out_specs=(anywhere, anywhere),
+        out_specs=(pl.BlockSpec(memory_space=pl.ANY),) * 2,
         scratch_shapes=scratch,
         compiler_params=pltpu.CompilerParams(
-            collective_id=0, has_side_effects=True, vmem_limit_bytes=60 * 1024 * 1024
+            collective_id=0, has_side_effects=True, vmem_limit_bytes=40 * 1024 * 1024
         ),
         name="ptychography",
-    )(row_offset, col_offset, objects, illumination, intensity, table, fresnel)
+    )(*[in_hbm(x) for x in (row_offset, col_offset, objects, illumination, intensity, table, fresnel)])
 
 
 def solution(mesh):

time: 63.2 us -> 59.6 us (0.943)
  Pallas kernels: 59.8 us -> 57.3 us
  local copies, waits for them, and re-layouts: 2.56 us -> 1.45 us
    pallas_call x1, Pallas kernels: 59.8 us -> 57.3 us  [on_device(): pl.pallas_call(functools.partial(kernel, mesh_shape), out_shape=(jax.Shap...]
    unnamed x4 -> x2, local copies, waits for them, and re-layouts: 2.56 us -> 1.45 us
where the time goes in v3:
time: 59.6 us; the launch traced here: 59.4 us
  Pallas kernels  57.3 us (96%)
  local copies, waits for them, and re-layouts  1.45 us (2%)
  between operations  0.64 us (1%)
    pallas_call x1, Pallas kernels, on_device(): pl.pallas_call(functools.partial(kernel, mesh_shape), out_shape=(jax.Shap...  57.3 us
    unnamed x2, local copies, waits for them, and re-layouts  1.45 us

profile of v3, /device:TPU:1, one launch (start us, length us, event | category | flops | bytes accessed | tf_op | source)
XLA Modules:
  0.0 59.4 jit_solution(10841342595109117445)
XLA Ops:
  0.6 57.3 %ptychography.1 = (f32[2,2,128,256]{3,2,1,0:T(8,128)S(1)}, f32[2,128,128]{2,1,0:T(8,128)S(1)}) custom-call(s32[4]{0:T(128)} %row_ref.1, s32[4]{0:T(128)} %col_ref.1, f32[2,2,128,256]{3,2,1,0:T(8,128)} %obj_ref.1, f32[2,128,128]{2,1,0:T(8,128)} %ill_ref.1, f32[4,128,128]{2,1,0:T(8,128)} %int_ref.1, bf16[4,256,256]{2,1,0:T(8,128)(2,1)} %constant.4.clone.tab_ref, ...), custom_call_target="tpu_custom_call" | custom-call | tf_op jit(solution)/shard_map/ptychography/pallas_call | solution.py:756
  58.0 0.8 %copy.11 = f32[2,2,128,256]{3,2,1,0:T(8,128)} copy(f32[2,2,128,256]{3,2,1,0:T(8,128)S(1)} %get-tuple-element.4) | data formatting | bytes 1048576
  58.8 0.7 %copy.12 = f32[2,128,128]{2,1,0:T(8,128)} copy(f32[2,128,128]{2,1,0:T(8,128)S(1)} %get-tuple-element.5) | data formatting | bytes 262144

commit v4 on v3

--- a/solution.py
+++ b/solution.py
@@ -373,8 +373,23 @@
                 def _(m=m):
                     relay_do(from_relay(phase, s, m))
 
-    def send_all(phase, s):
-        each(phase, s, lambda copy: copy.start())
+    def send_far(phase, s):
+        for m in order:
+            if messages[m][0][0]:
+
+                @pl.when(also(sends(m), leaves_group(m)))
+                def _(m=m):
+                    (to_relay if relayed(m) else straight)(phase, s, m).start()
+
+    def send_near(phase, s):
+        for m in order:
+            flag = sends(m)
+            if messages[m][0][0]:
+                flag = also(flag, jnp.logical_not(leaves_group(m)))
+
+            @pl.when(flag)
+            def _(m=m):
+                straight(phase, s, m).start()
 
     def pass_on(phase, s):
         for m in range(len(messages)):
@@ -410,11 +425,13 @@
         )
 
     pack_edges(0)
+    pack_edges(1)
     pl.semaphore_wait(barrier, expected)
-    send_all(0, 0)
+    send_far(0, 0)
+    send_far(0, 1)
+    send_near(0, 0)
     second_stage()
-    pack_edges(1)
-    send_all(0, 1)
+    send_near(0, 1)
 
     row_at = [row_ref[j] for j in range(count)]
     col_at = [col_ref[j] for j in range(count)]
@@ -662,17 +679,19 @@
 
     start_many(scatter_copy, inner_steps[:-1])
     place(1, conj_times(moved_s[...], exit_grad))
-    send_all(1, 1)
     place(0, conj_times(probe, entry_grad))
-    send_all(1, 0)
 
     ar_in[rows_of(my_inner)] = ar_src[rows_of(my_inner)]
-    pass_on(1, 1)
-    pass_on(1, 0)
     wait_many(ar_in, inner, ar_recv.at[0])
     z_in[rows_of(my_outer)] = sum(ar_in[k * chunk : (k + 1) * chunk] for k in range(inner))
     last_stage()
     start_many(outer_copy, outer_steps)
+    send_far(1, 1)
+    send_far(1, 0)
+    send_near(1, 1)
+    send_near(1, 0)
+    pass_on(1, 1)
+    pass_on(1, 0)
 
 
     wait_many(z_in, outer, ar_recv.at[1])
@@ -687,6 +706,11 @@
     receive_all(1, 0)
     finish(0)
 
+    wait_many(ar_src, inner, ar_send.at[0])
+    wait_many(z_in, outer, ar_send.at[1])
+    for s in range(2):
+        sent_all(0, s)
+        sent_all(1, s)
     wait_many(ar_out, inner, ar_recv.at[2])
     probe_copies = [
         pltpu.make_async_copy(
@@ -696,12 +720,8 @@
     ]
     for copy in probe_copies:
         copy.start()
-    wait_many(ar_src, inner, ar_send.at[0])
-    wait_many(z_in, outer, ar_send.at[1])
     wait_many(ar_out, inner, ar_send.at[2])
     for s in range(2):
-        sent_all(0, s)
-        sent_all(1, s)
         out_copy(s).wait()
     for copy in probe_copies:
         copy.wait()

time: 59.6 us -> 56.3 us (0.945)
  Pallas kernels: 57.3 us -> 53.7 us
    pallas_call x1, Pallas kernels: 57.3 us -> 53.7 us  [on_device(): pl.pallas_call(functools.partial(kernel, mesh_shape), out_shape=(jax.Shap...]
where the time goes in v4:
time: 56.3 us; the launch traced here: 55.8 us
  Pallas kernels  53.7 us (95%)
  local copies, waits for them, and re-layouts  1.45 us (3%)
  between operations  0.64 us (1%)
    pallas_call x1, Pallas kernels, on_device(): pl.pallas_call(functools.partial(kernel, mesh_shape), out_shape=(jax.Shap...  53.7 us
    unnamed x2, local copies, waits for them, and re-layouts  1.45 us

profile of v4, /device:TPU:1, one launch (start us, length us, event | category | flops | bytes accessed | tf_op | source)
XLA Modules:
  0.0 55.8 jit_solution(16568678796734750587)
XLA Ops:
  0.6 53.7 %ptychography.1 = (f32[2,2,128,256]{3,2,1,0:T(8,128)S(1)}, f32[2,128,128]{2,1,0:T(8,128)S(1)}) custom-call(s32[4]{0:T(128)} %row_ref.1, s32[4]{0:T(128)} %col_ref.1, f32[2,2,128,256]{3,2,1,0:T(8,128)} %obj_ref.1, f32[2,128,128]{2,1,0:T(8,128)} %ill_ref.1, f32[4,128,128]{2,1,0:T(8,128)} %int_ref.1, bf16[4,256,256]{2,1,0:T(8,128)(2,1)} %constant.4.clone.tab_ref, ...), custom_call_target="tpu_custom_call" | custom-call | tf_op jit(solution)/shard_map/ptychography/pallas_call | solution.py:776
  54.3 0.8 %copy.11 = f32[2,2,128,256]{3,2,1,0:T(8,128)} copy(f32[2,2,128,256]{3,2,1,0:T(8,128)S(1)} %get-tuple-element.4) | data formatting | bytes 1048576
  55.1 0.7 %copy.12 = f32[2,128,128]{2,1,0:T(8,128)} copy(f32[2,128,128]{2,1,0:T(8,128)S(1)} %get-tuple-element.5) | data formatting | bytes 262144

commit v5 on v4

--- a/solution.py
+++ b/solution.py
@@ -604,10 +604,10 @@
     probe = jnp.concatenate([illumination] * count, axis=0)
 
     pass_on(0, 0)
+    pass_on(0, 1)
     receive_all(0, 0)
     join_halo(0)
     gather(0, first_w)
-    pass_on(0, 1)
     third_stage()
     moved_s[...] = propagate(times(probe, first_w[...]), 1.0)
 
@@ -682,9 +682,9 @@
     place(0, conj_times(probe, entry_grad))
 
     ar_in[rows_of(my_inner)] = ar_src[rows_of(my_inner)]
+    last_stage()
     wait_many(ar_in, inner, ar_recv.at[0])
     z_in[rows_of(my_outer)] = sum(ar_in[k * chunk : (k + 1) * chunk] for k in range(inner))
-    last_stage()
     start_many(outer_copy, outer_steps)
     send_far(1, 1)
     send_far(1, 0)

time: 56.3 us -> 56.1 us (level)
  no operation moved by 1% of the time
where the time goes in v5:
time: 56.1 us; the launch traced here: 55.9 us
  Pallas kernels  53.9 us (96%)
  local copies, waits for them, and re-layouts  1.45 us (3%)
  between operations  0.64 us (1%)
    pallas_call x1, Pallas kernels, on_device(): pl.pallas_call(functools.partial(kernel, mesh_shape), out_shape=(jax.Shap...  53.9 us
    unnamed x2, local copies, waits for them, and re-layouts  1.45 us

profile of v5, /device:TPU:1, one launch (start us, length us, event | category | flops | bytes accessed | tf_op | source)
XLA Modules:
  0.0 55.9 jit_solution(13719466046321266287)
XLA Ops:
  0.6 53.9 %ptychography.1 = (f32[2,2,128,256]{3,2,1,0:T(8,128)S(1)}, f32[2,128,128]{2,1,0:T(8,128)S(1)}) custom-call(s32[4]{0:T(128)} %row_ref.1, s32[4]{0:T(128)} %col_ref.1, f32[2,2,128,256]{3,2,1,0:T(8,128)} %obj_ref.1, f32[2,128,128]{2,1,0:T(8,128)} %ill_ref.1, f32[4,128,128]{2,1,0:T(8,128)} %int_ref.1, bf16[4,256,256]{2,1,0:T(8,128)(2,1)} %constant.4.clone.tab_ref, ...), custom_call_target="tpu_custom_call" | custom-call | tf_op jit(solution)/shard_map/ptychography/pallas_call | solution.py:776
  54.5 0.8 %copy.11 = f32[2,2,128,256]{3,2,1,0:T(8,128)} copy(f32[2,2,128,256]{3,2,1,0:T(8,128)S(1)} %get-tuple-element.4) | data formatting | bytes 1048576
  55.3 0.7 %copy.12 = f32[2,128,128]{2,1,0:T(8,128)} copy(f32[2,128,128]{2,1,0:T(8,128)S(1)} %get-tuple-element.5) | data formatting | bytes 262144
